TPU v7x, 128 devices: a whole 4x4x4 slice. The times are simulated.
128 devices in a mesh: worker: 16 (over x_lo, z, core), fsdp: 8 (over x_hi, y).
Axes of the slice: x: 4 (x_hi: 2, x_lo: 2; x = x_hi * 2 + x_lo), y: 4, z: 4, core: 2. Of those that a mesh axis runs over, the one named last changes fastest.
Arguments:
- tokens_x: bfloat16 [16384, 4096], P(('worker', 'fsdp')), may hold values from -24 to 24
- attn_out: bfloat16 [16384, 2048], P(('worker', 'fsdp')), may hold values from -24 to 24
- query_cot: bfloat16 [16384, 2048], P(('worker', 'fsdp')), may hold values from -0.5 to 0.5
- out_cot: bfloat16 [16384, 4096], P(('worker', 'fsdp')), may hold values from -0.5 to 0.5
- message_ids: int32 [16384], P(('worker', 'fsdp')), may hold values from 0 to 1023
- q_offset: float32 [16, 4096, 2048], P('worker', 'fsdp'), may hold values from -12 to 12
- q_first: bfloat16 [16, 4096, 2048], P('worker', 'fsdp'), may hold values from -1.5 to 1.5
- q_second: bfloat16 [16, 4096, 2048], P('worker', 'fsdp'), may hold values from 0.0009994507 to 0.099609375
- o_offset: float32 [16, 2048, 4096], P('worker', 'fsdp'), may hold values from -12 to 12
- o_first: bfloat16 [16, 2048, 4096], P('worker', 'fsdp'), may hold values from -1.5 to 1.5
- o_second: bfloat16 [16, 2048, 4096], P('worker', 'fsdp'), may hold values from 0.0009994507 to 0.099609375
- q_momentum: float32 [4096, 2048], P(('fsdp', 'worker')), may hold values from -6 to 6
- o_momentum: float32 [2048, 4096], P(('fsdp', 'worker')), may hold values from -6 to 6
Outputs:
- q_first_new: bfloat16 [16, 4096, 2048], P('worker', 'fsdp')
- o_first_new: bfloat16 [16, 2048, 4096], P('worker', 'fsdp')
- q_direction: float32 [4096, 2048], P(('fsdp', 'worker'))
- o_direction: float32 [2048, 4096], P(('fsdp', 'worker'))
- q_momentum_new: float32 [4096, 2048], P(('fsdp', 'worker'))
- o_momentum_new: float32 [2048, 4096], P(('fsdp', 'worker'))
All inputs are finite; a program needn't handle non-finite values.
Results may differ from a plain program's by a relative error of at most 0.019.
Values may be sent and summed in bfloat16 or wider, within the bound.
A program may use at most 192 MiB of HBM per device.

v0:
```python
import jax
import jax.numpy as jnp
from jax import lax
from jax.sharding import PartitionSpec as P

CONTROL = 256
STEP = 500


first_decay = 0.9
second_decay = 0.999
adam_eps = 1e-08
outer_mu = 0.9


def cross_rows(left, right):
    return lax.dot_general(
        left, right, (((0,), (0,)), ((), ())), preferred_element_type=jnp.float32
    )


def rounded(part):
    return lax.optimization_barrier(part.astype(jnp.bfloat16)).astype(jnp.float32)


def adam_moved(grads, offset, first, second):
    first_new = first_decay * first.astype(jnp.float32) + (1.0 - first_decay) * grads
    second_new = second_decay * second.astype(jnp.float32) + (1.0 - second_decay) * grads * grads
    first_hat = first_new / (1.0 - first_decay**STEP)
    second_hat = second_new / (1.0 - second_decay**STEP)
    moved = offset + first_hat / (jnp.sqrt(second_hat) + adam_eps)
    return (first_new.astype(jnp.bfloat16), moved)


def per_device(
    tokens_x,
    attn_out,
    query_cot,
    out_cot,
    message_ids,
    q_offset,
    q_first,
    q_second,
    o_offset,
    o_first,
    o_second,
    q_momentum,
    o_momentum,
):
    loss_mask = (message_ids >= CONTROL).astype(jnp.bfloat16)[:, None]
    q_cot = query_cot * loss_mask
    o_cot = out_cot * loss_mask
    tok_rows = tokens_x.shape[0]
    rows_q = q_offset.shape[1]
    rows_o = o_offset.shape[1]
    x_cols, a_cols = (
        lax.all_to_all(tokens_x, "fsdp", split_axis=1, concat_axis=0, tiled=True),
        lax.all_to_all(attn_out, "fsdp", split_axis=1, concat_axis=0, tiled=True),
    )
    first_row = jnp.int32(0)
    piece_q = lax.all_gather(q_cot, "fsdp", axis=0, tiled=True)
    piece_o = lax.all_gather(o_cot, "fsdp", axis=0, tiled=True)
    grads_q = jnp.zeros((rows_q, q_offset.shape[2]), jnp.float32)
    grads_o = jnp.zeros((rows_o, o_offset.shape[2]), jnp.float32)
    for number in range(piece_q.shape[0] // tok_rows):
        row = first_row + number * tok_rows
        left_q = lax.dynamic_slice_in_dim(x_cols, row, tok_rows, 0)
        left_o = lax.dynamic_slice_in_dim(a_cols, row, tok_rows, 0)
        right_q = piece_q[number * tok_rows : (number + 1) * tok_rows]
        right_o = piece_o[number * tok_rows : (number + 1) * tok_rows]
        grads_q = grads_q + rounded(cross_rows(left_q, right_q))
        grads_o = grads_o + rounded(cross_rows(left_o, right_o))
    q_first_new, moved_q = adam_moved(grads_q, q_offset[0], q_first[0], q_second[0])
    o_first_new, moved_o = adam_moved(grads_o, o_offset[0], o_first[0], o_second[0])
    workers = lax.axis_size("worker")
    total_q, total_o = (
        lax.psum(moved_q.astype(jnp.bfloat16), "worker").astype(jnp.float32),
        lax.psum(moved_o.astype(jnp.bfloat16), "worker").astype(jnp.float32),
    )
    worker_pos = lax.axis_index("worker")
    share_rows_q = rows_q // workers
    share_rows_o = rows_o // workers
    share_q = lax.dynamic_slice_in_dim(total_q, worker_pos * share_rows_q, share_rows_q, 0)
    share_o = lax.dynamic_slice_in_dim(total_o, worker_pos * share_rows_o, share_rows_o, 0)
    pseudo_q = share_q / workers
    pseudo_o = share_o / workers
    q_momentum_new = outer_mu * q_momentum + pseudo_q
    o_momentum_new = outer_mu * o_momentum + pseudo_o
    q_direction = pseudo_q + outer_mu * q_momentum_new
    o_direction = pseudo_o + outer_mu * o_momentum_new
    return (
        q_first_new[None],
        o_first_new[None],
        q_direction,
        o_direction,
        q_momentum_new,
        o_momentum_new,
    )


def solution(mesh):
    in_specs = (
        P(("worker", "fsdp"), None),
        P(("worker", "fsdp"), None),
        P(("worker", "fsdp"), None),
        P(("worker", "fsdp"), None),
        P(("worker", "fsdp")),
        P("worker", "fsdp", None),
        P("worker", "fsdp", None),
        P("worker", "fsdp", None),
        P("worker", "fsdp", None),
        P("worker", "fsdp", None),
        P("worker", "fsdp", None),
        P(("fsdp", "worker"), None),
        P(("fsdp", "worker"), None),
    )
    out_specs = (
        P("worker", "fsdp", None),
        P("worker", "fsdp", None),
        P(("fsdp", "worker"), None),
        P(("fsdp", "worker"), None),
        P(("fsdp", "worker"), None),
        P(("fsdp", "worker"), None),
    )
    return jax.shard_map(
        per_device, mesh=mesh, in_specs=in_specs, out_specs=out_specs, check_vma=False
    )
```

profile of v0, /device:TPU:1, one launch (start us, length us, event | category | flops | bytes accessed | tf_op | source)
XLA Modules:
  0.0 372.3 jit_solution(17039477943532699633)
XLA Ops:
  10.0 2.5 broadcast_multiply_fusion
  13.8 7.5 %all-to-all-start = ((bf16[128,8,512]{0,2,1:T(8,128)(2,1)}), bf16[128,8,512]{0,2,1:T(8,128)(2,1)S(1)}, u32[]{:S(2)}, u32[]{:S(2)}) async-start(bf16[128,8,512]{0,2,1:T(8,128)(2,1)} %bitcast.1), calls=%async_computation | async-start | bytes 2097152 | tf_op jit(solution)/shard_map/all_to_all | solution.py:57
  22.3 3.3 copy.59
  25.6 5.6 %copy.72 = f32[1,256,4096]{1,2,0:T(8,128)} copy(f32[1,256,4096]{2,1,0:T(8,128)} %param.21) | data formatting | bytes 8388608 | tf_op args[8]
  31.3 4.1 %copy.73 = bf16[1,256,4096]{1,2,0:T(8,128)(2,1)} copy(bf16[1,256,4096]{2,1,0:T(8,128)(2,1)} %param.23) | data formatting | bytes 4194304 | tf_op args[10]
  35.4 3.9 %copy.49 = bf16[1,512,2048]{1,2,0:T(8,128)(2,1)} copy(bf16[1,512,2048]{2,1,0:T(8,128)(2,1)} %param.19) | data formatting | bytes 4194304 | tf_op args[6]
  39.3 5.4 %copy.69 = f32[1,512,2048]{1,2,0:T(8,128)} copy(f32[1,512,2048]{2,1,0:T(8,128)} %param.18) | data formatting | bytes 8388608 | tf_op args[5]
  44.7 3.9 %copy.70 = bf16[1,512,2048]{1,2,0:T(8,128)(2,1)} copy(bf16[1,512,2048]{2,1,0:T(8,128)(2,1)} %param.20) | data formatting | bytes 4194304 | tf_op args[7]
  48.6 6.6 %all-to-all-start.1 = ((bf16[128,8,256]{0,2,1:T(8,128)(2,1)}), bf16[128,8,256]{0,2,1:T(8,128)(2,1)}, u32[]{:S(2)}, u32[]{:S(2)}) async-start(bf16[128,8,256]{0,2,1:T(8,128)(2,1)} %bitcast.148), calls=%async_computation.1 | async-start | bytes 1048576 | tf_op jit(solution)/shard_map/all_to_all | solution.py:58
  55.3 40.8 %all-gather.3.cloned.1.call-done = bf16[1024,2048]{1,0:T(8,128)(2,1)} async-done(((bf16[128,2048]{1,0:T(8,128)(2,1)}), bf16[1024,2048]{1,0:T(8,128)(2,1)}) %all-gather.3.cloned.1.call-update) | async-done | bytes 4194320 | tf_op jit(solution)/shard_map/all_gather | solution.py:61
  104.8 3.1 fusion.31
  107.9 8.4 %fusion.23 = (bf16[512,2048]{0,1:T(8,128)(2,1)}, f32[512,2048]{0,1:T(8,128)}) fusion(bf16[1,512,2048]{1,2,0:T(8,128)(2,1)S(1)} %copy-done.6, bf16[1,512,2048]{1,2,0:T(8,128)(2,1)S(1)} %copy-done, f32[1,512,2048]{1,2,0:T(8,128)S(1)} %copy-done.2, bf16[512,2048]{0,1:T(8,128)(2,1)} %fusion.31, bf16[512,2048]{0,1:T(8,128)(2,1)S(1)} %fusion.30, ...), kind=kLoop, calls=%fused_computation.37 | loop fusion | flops 30408704 | bytes 31457280 | tf_op jit(solution)/shard_map/convert_element_type | solution.py:77
  116.3 87.1 %all-gather.5.cloned.1.call-done = bf16[1024,4096]{1,0:T(8,128)(2,1)} async-done(((bf16[128,4096]{1,0:T(8,128)(2,1)}), bf16[1024,4096]{1,0:T(8,128)(2,1)}) %all-gather.5.cloned.1.call-update) | async-done | bytes 8388624 | tf_op jit(solution)/shard_map/all_gather | solution.py:62
  203.4 2.1 fusion
  205.5 2.5 fusion.1
  218.2 6.9 %fusion.22 = (bf16[256,4096]{0,1:T(8,128)(2,1)}, f32[256,4096]{0,1:T(8,128)}) fusion(bf16[1,256,4096]{1,2,0:T(8,128)(2,1)S(1)} %copy-done.5, bf16[1,256,4096]{1,2,0:T(8,128)(2,1)S(1)} %copy.59, f32[1,256,4096]{1,2,0:T(8,128)S(1)} %copy-done.1, bf16[256,4096]{0,1:T(8,128)(2,1)S(1)} %fusion.7, bf16[256,4096]{0,1:T(8,128)(2,1)S(1)} %fusion.6, ...), kind=kLoop, calls=%fused_computation.36 | loop fusion | flops 30408704 | bytes 31457280 | tf_op jit(solution)/shard_map/convert_element_type | solution.py:78
  228.4 5.0 %fusion.32 = bf16[1,512,2048]{1,2,0:T(8,128)(2,1)} fusion(f32[512,2048]{0,1:T(8,128)} %get-tuple-element.33, bf16[1,512,2048]{1,2,0:T(8,128)(2,1)} %copy.49), kind=kLoop, calls=%fused_computation.54 | loop fusion | flops 5242880 | bytes 8388608 | tf_op jit(solution)/shard_map/broadcast_in_dim | solution.py:92
  233.4 3.9 %copy.76 = bf16[1,512,2048]{2,1,0:T(8,128)(2,1)} copy(bf16[1,512,2048]{1,2,0:T(8,128)(2,1)} %fusion.32) | data formatting | bytes 4194304
  237.3 4.2 %fusion.33 = bf16[1,256,4096]{1,2,0:T(8,128)(2,1)} fusion(f32[256,4096]{0,1:T(8,128)} %get-tuple-element.31, bf16[1,256,4096]{1,2,0:T(8,128)(2,1)S(1)} %copy.59), kind=kLoop, calls=%fused_computation.55 | loop fusion | flops 5242880 | bytes 8388608 | tf_op jit(solution)/shard_map/broadcast_in_dim | solution.py:93
  241.4 4.2 %copy.77 = bf16[1,256,4096]{2,1,0:T(8,128)(2,1)} copy(bf16[1,256,4096]{1,2,0:T(8,128)(2,1)} %fusion.33) | data formatting | bytes 4194304
  245.7 107.3 %all-reduce.3.cloned.1.call-done = (bf16[512,2048]{0,1:T(8,128)(2,1)}, bf16[256,4096]{0,1:T(8,128)(2,1)}) async-done(((bf16[512,2048]{0,1:T(8,128)(2,1)}, bf16[256,4096]{0,1:T(8,128)(2,1)}), (bf16[512,2048]{0,1:T(8,128)(2,1)}, bf16[256,4096]{0,1:T(8,128)(2,1)})) %all-reduce.3.cloned.1.call-update) | async-done | bytes 4194320 | tf_op jit(solution)/shard_map/psum | solution.py:77
  352.9 3.7 %multiply_add_fusion = (f32[16,4096]{0,1:T(8,128)}, f32[16,4096]{0,1:T(8,128)}) fusion(bf16[256,4096]{0,1:T(8,128)(2,1)} %get-tuple-element.25, s32[]{:T(128)S(6)} %select_n.7, f32[16,4096]{0,1:T(8,128)S(1)} %copy-done.4), kind=kLoop, calls=%fused_computation.56 | loop fusion | flops 327680 | bytes 917508 | tf_op jit(solution)/shard_map/add | solution.py:90
  356.7 2.9 copy.79
  359.5 2.9 copy.81
  (57 shorter events, 30.6 us)
Async XLA Ops:
  7.2 5.3 %copy-start.9 = (bf16[128,4096]{1,0:T(8,128)(2,1)S(1)}, bf16[128,4096]{1,0:T(8,128)(2,1)}, u32[]{:S(2)}) copy-start(bf16[128,4096]{1,0:T(8,128)(2,1)} %param.13) | copy-start | bytes 3145732
  7.2 88.9 %all-gather.3.cloned.1.call-start = ((), (), s32[]{:S(2)}) async-start(), calls=%async_computation.2 | async-start | bytes 4718592 | tf_op jit(solution)/shard_map/all_gather | solution.py:61
  9.9 11.4 %copy-start.10 = (bf16[128,2048]{1,0:T(8,128)(2,1)S(1)}, bf16[128,2048]{1,0:T(8,128)(2,1)}, u32[]{:S(2)}) copy-start(bf16[128,2048]{1,0:T(8,128)(2,1)} %param.14) | copy-start | bytes 1572868
  9.9 193.4 %all-gather.5.cloned.1.call-start = ((), (), s32[]{:S(2)}) async-start(), calls=%async_computation.3 | async-start | bytes 9437184 | tf_op jit(solution)/shard_map/all_gather | solution.py:62
  13.8 34.8 %all-to-all-start = ((bf16[128,8,512]{0,2,1:T(8,128)(2,1)}), bf16[128,8,512]{0,2,1:T(8,128)(2,1)S(1)}, u32[]{:S(2)}, u32[]{:S(2)}) async-start(bf16[128,8,512]{0,2,1:T(8,128)(2,1)} %bitcast.1), calls=%async_computation | async-start | bytes 2097152 | tf_op jit(solution)/shard_map/all_to_all | solution.py:57
  48.6 53.5 %copy-start.8 = (bf16[128,8,512]{0,2,1:T(8,128)(2,1)}, bf16[128,8,512]{0,2,1:T(8,128)(2,1)S(1)}, u32[]{:S(2)}) copy-start(bf16[128,8,512]{0,2,1:T(8,128)(2,1)S(1)} %all-to-all-done) | copy-start | bytes 3145732
  48.6 67.7 %all-to-all-start.1 = ((bf16[128,8,256]{0,2,1:T(8,128)(2,1)}), bf16[128,8,256]{0,2,1:T(8,128)(2,1)}, u32[]{:S(2)}, u32[]{:S(2)}) async-start(bf16[128,8,256]{0,2,1:T(8,128)(2,1)} %bitcast.148), calls=%async_computation.1 | async-start | bytes 1048576 | tf_op jit(solution)/shard_map/all_to_all | solution.py:58
  55.2 297.7 %all-reduce.3.cloned.1.call-start = ((), (), s32[]{:S(2)}) async-start(), calls=%async_computation.4 | async-start | bytes 8388608 | tf_op jit(solution)/shard_map/psum | solution.py:77
  96.1 3.7 copy-start.7
  101.3 6.6 %copy-start.6 = (bf16[1,512,2048]{1,2,0:T(8,128)(2,1)S(1)}, bf16[1,512,2048]{1,2,0:T(8,128)(2,1)}, u32[]{:S(2)}) copy-start(bf16[1,512,2048]{1,2,0:T(8,128)(2,1)} %copy.70) | copy-start | bytes 6291460
  102.1 5.8 %copy-start = (bf16[1,512,2048]{1,2,0:T(8,128)(2,1)S(1)}, bf16[1,512,2048]{1,2,0:T(8,128)(2,1)}, u32[]{:S(2)}) copy-start(bf16[1,512,2048]{1,2,0:T(8,128)(2,1)} %copy.49) | copy-start | bytes 6291460
  102.1 5.8 %copy-start.2 = (f32[1,512,2048]{1,2,0:T(8,128)S(1)}, f32[1,512,2048]{1,2,0:T(8,128)}, u32[]{:S(2)}) copy-start(f32[1,512,2048]{1,2,0:T(8,128)} %copy.69) | copy-start | bytes 12582916
  203.4 6.6 %copy-start.3 = (bf16[1024,4096]{1,0:T(8,128)(2,1)S(1)}, bf16[1024,4096]{1,0:T(8,128)(2,1)}, u32[]{:S(2)}) copy-start(bf16[1024,4096]{1,0:T(8,128)(2,1)} %all-gather.5.cloned.1.call-done) | copy-start | bytes 25165828
  213.1 5.1 %copy-start.1 = (f32[1,256,4096]{1,2,0:T(8,128)S(1)}, f32[1,256,4096]{1,2,0:T(8,128)}, u32[]{:S(2)}) copy-start(f32[1,256,4096]{1,2,0:T(8,128)} %copy.72) | copy-start | bytes 12582916
  213.1 5.1 %copy-start.5 = (bf16[1,256,4096]{1,2,0:T(8,128)(2,1)S(1)}, bf16[1,256,4096]{1,2,0:T(8,128)(2,1)}, u32[]{:S(2)}) copy-start(bf16[1,256,4096]{1,2,0:T(8,128)(2,1)} %copy.73) | copy-start | bytes 6291460
  225.1 0.9 copy-start.12
  225.1 2.9 copy-start.11
  241.4 111.5 %copy-start.4 = (f32[16,4096]{0,1:T(8,128)S(1)}, f32[16,4096]{0,1:T(8,128)}, u32[]{:S(2)}) copy-start(f32[16,4096]{0,1:T(8,128)} %copy.75) | copy-start | bytes 786436
Sparse Core Ops, SparseCore 0:
  10.4 85.6 all-gather.2
  98.5 104.8 all-gather.4
  225.3 127.6 all-reduce.2
where the time goes:
time: 374 us; the launch traced here: 372 us
  waiting for transfers between devices  235 us (63%)
  local copies, waits for them, and re-layouts  47.8 us (13%)
  other arithmetic  34.6 us (9%)
  matrix products  26.4 us (7%)
  starting transfers between devices  14.2 us (4%)
  between operations  14 us (4%)
    psum x1, waiting for transfers between devices, per_device(): lax.psum(moved_q.astype(jnp.bfloat16), 'worker').astype(jnp.float32)  107 us
    all_gather x1, waiting for transfers between devices, per_device(): piece_o = lax.all_gather(o_cot, 'fsdp', axis=0, tiled=True)  87.1 us
    unnamed x41, local copies, waits for them, and re-layouts  45.8 us
    all_gather x1, waiting for transfers between devices, per_device(): piece_q = lax.all_gather(q_cot, 'fsdp', axis=0, tiled=True)  40.8 us
    dot_general x16, matrix products, cross_rows(): lax.dot_general(left, right, (((0,), (0,)), ((), ())), preferred_element_...  26.4 us
    convert_element_type x1, other arithmetic, per_device(): moved_q.astype(jnp.bfloat16)  8.37 us
    all_to_all x1, starting transfers between devices, per_device(): lax.all_to_all(tokens_x, 'fsdp', split_axis=1, concat_axis=0, tiled=True)  7.48 us
  transfers between devices with their start and end apart: 5, of which 3 were waited for; matrix products, arithmetic and copies ran while one was open for 19% of the time, Pallas kernels for 0%

commit v1 on v0

v1 whole, which is shorter than its diff:
```python
import jax
import jax.numpy as jnp
from jax import lax
from jax.experimental import pallas as pl
from jax.experimental.pallas import tpu as pltpu
from jax.sharding import PartitionSpec as P

CONTROL = 256
STEP = 500
TOK = 128

first_decay = 0.9
second_decay = 0.999
adam_eps = 1e-08
outer_mu = 0.9
workers = 16
first_fix = 1.0 / (1.0 - first_decay**STEP)
second_fix = 1.0 / (1.0 - second_decay**STEP)

f32, bf16 = jnp.float32, jnp.bfloat16
MESH = pl.DeviceIdType.MESH

CHUNKS = tuple(
    (kind, number * width, width) for number in range(8) for kind, width in (("q", 256), ("o", 512))
)
AHEAD = 4
FORWARD = 2
LATER = (3, 4, 6, 8)
GATHER, HALF, CORE, ZED, XLO, OWN = 0, 3, 4, 5, 8, 9
N_SEM = 10


class Side:
    pass


def kernel(*refs):
    n_in, n_out = 13, 6
    ids_ref, x_hbm, a_hbm, cq_hbm, co_hbm = refs[:5]
    qoff_hbm, qfir_hbm, qsec_hbm, ooff_hbm, ofir_hbm, osec_hbm, qmom_hbm, omom_hbm = refs[5:n_in]
    scratch = refs[n_in + n_out :]
    x_in, a_in, x_t, a_t, lhs_send, lhs_recv, load_sem, send_sem, recv_sem = scratch[:9]
    names = ("lhs", "cot", "half_s", "half_r", "grad", "off", "sec", "core_r", "z_s", "z_r", "x_s", "x_r", "mine")
    q, o = Side(), Side()
    for place, name in enumerate(names):
        setattr(q, name, scratch[9 + place])
        setattr(o, name, scratch[9 + len(names) + place])
    q.cot_hbm, o.cot_hbm = cq_hbm, co_hbm
    q.fir, o.fir, q.way, o.way, q.mom, o.mom = refs[n_in : n_in + n_out]

    w, f = lax.axis_index("worker"), lax.axis_index("fsdp")
    core, z, xl = w % 2, (w // 2) % 4, w // 8
    y, xh = f % 4, f // 4

    def device(xl=xl, z=z, core=core, xh=xh, y=y):
        return (xl * 8 + z * 2 + core, xh * 4 + y)

    ring = [device(y=(y + k) % 4) for k in (1, 2, 3)]
    across = device(xh=1 - xh)
    beside = device(y=3 - y)
    corner = device(xh=1 - xh, y=3 - y)
    halver = device(y=y + 1 - 2 * (y % 2))
    twin = device(core=1 - core)
    zeds = [device(z=(z + k) % 4) for k in (1, 2, 3)]
    near = device(xl=1 - xl)

    q.own, q.other, q.partner = xh, 1 - xh, across
    o.own, o.other, o.partner = y % 2, 1 - y % 2, halver
    q.slot, o.slot = y, xh * 2 + y // 2

    loads = [
        pltpu.make_async_copy(a, b, load_sem.at[i])
        for i, (a, b) in enumerate(
            (
                (a_hbm, a_in),
                (x_hbm, x_in),
                (ooff_hbm, o.off),
                (ofir_hbm, o.fir),
                (osec_hbm, o.sec),
                (qoff_hbm, q.off),
                (qfir_hbm, q.fir),
                (qsec_hbm, q.sec),
                (omom_hbm, o.mom),
                (qmom_hbm, q.mom),
            )
        )
    ]
    for load in loads[:2]:
        load.start()

    barrier = pltpu.get_barrier_semaphore()
    met = (*ring, across, corner, twin, *zeds, near)
    for other in met:
        pl.semaphore_signal(barrier, inc=1, device_id=other, device_id_type=MESH)

    def own_block(side, number, c0, cw):
        return pltpu.make_async_copy(
            side.cot_hbm.at[:, pl.ds(c0, cw)],
            side.cot.at[pl.ds(pl.multiple_of(side.slot * TOK, TOK), TOK), pl.ds(c0, cw)],
            recv_sem.at[number, OWN],
        )

    own_copies = [own_block(q if kind == "q" else o, n, c0, cw) for n, (kind, c0, cw) in enumerate(CHUNKS)]
    for copy in own_copies:
        copy.start()
    for load in loads[2:]:
        load.start()

    mask = (ids_ref[...] >= CONTROL).astype(f32)
    loads[0].wait()

    @pl.loop(0, 8)
    def _(part):
        rows = a_in[:, pl.ds(pl.multiple_of(part * 256, 256), 256)].astype(f32)
        a_t[part // 4, part % 4] = (rows.T * mask).astype(bf16)

    loads[1].wait()

    @pl.loop(0, 8)
    def _(part):
        rows = x_in[:, pl.ds(pl.multiple_of(part * 512, 512), 512)].astype(f32)
        x_t[part // 4, part % 4] = (rows.T * mask).astype(bf16)

    def lanes(slot):
        return pl.ds(pl.multiple_of(slot * TOK, TOK), TOK)

    mine = [
        pltpu.make_async_copy(a_t.at[xh, pl.ds(2 * (y // 2), 2)], o.lhs.at[:, :, lanes(o.slot)], lhs_send.at[6]),
        pltpu.make_async_copy(x_t.at[:, y], q.lhs.at[:, :, lanes(q.slot)], lhs_send.at[7]),
    ]
    for copy in mine:
        copy.start()

    pl.semaphore_wait(barrier, len(met))

    sent = []

    def send(src, dst, s, r, to):
        copy = pltpu.make_async_remote_copy(
            src_ref=src, dst_ref=dst, send_sem=s, recv_sem=r, device_id=to, device_id_type=MESH
        )
        copy.start()
        sent.append(copy)
        return copy

    o_lhs, q_lhs = [], []

    def send_o_lhs():
        for i, (to, xt, yt) in enumerate(((across, 1 - xh, y), (beside, xh, 3 - y), (corner, 1 - xh, 3 - y))):
            o_lhs.append(
                send(
                    a_t.at[xt, pl.ds(2 * (yt // 2), 2)],
                    o.lhs.at[:, :, lanes(o.slot)],
                    lhs_send.at[i],
                    lhs_recv.at[i],
                    to,
                )
            )

    def send_q_lhs():
        for i, to in enumerate(ring):
            q_lhs.append(
                send(
                    x_t.at[:, (y + i + 1) % 4],
                    q.lhs.at[:, :, lanes(q.slot)],
                    lhs_send.at[3 + i],
                    lhs_recv.at[3 + i],
                    to,
                )
            )

    gathers = {}
    halves, cores, zs, xs = {}, {}, {}, {}

    def gather(n):
        kind, c0, cw = CHUNKS[n]
        side = q if kind == "q" else o
        cols = pl.ds(c0, cw)
        src = side.cot_hbm.at[:, cols]
        dst = side.cot.at[pl.ds(pl.multiple_of(side.slot * TOK, TOK), TOK), cols]
        targets = ring if kind == "q" else (across, beside)
        gathers[n] = [
            send(src, dst, send_sem.at[n, GATHER + i], recv_sem.at[n, GATHER + i], to) for i, to in enumerate(targets)
        ]

    def forward(n):
        kind, c0, cw = CHUNKS[n]
        if kind == "q":
            return
        gathers[n][0].wait_recv()
        slot = (1 - xh) * 2 + y // 2
        block = o.cot.at[pl.ds(pl.multiple_of(slot * TOK, TOK), TOK), pl.ds(c0, cw)]
        gathers[n].append(send(block, block, send_sem.at[n, GATHER + 2], recv_sem.at[n, GATHER + 2], beside))

    def product(side, which, c0, cw, store):
        @pl.loop(0, cw // 256)
        def _(part):
            there = pl.ds(pl.multiple_of(c0 + part * 256, 256), 256)
            here = pl.ds(pl.multiple_of(part * 256, 256), 256)
            store(there, here, jnp.dot(side.lhs[which], side.cot[:, there], preferred_element_type=f32))

    lhs_ready = set()

    def partial(n):
        kind, c0, cw = CHUNKS[n]
        side = q if kind == "q" else o
        if kind not in lhs_ready:
            lhs_ready.add(kind)
            mine[1 if kind == "q" else 0].wait()
            for copy in q_lhs if kind == "q" else o_lhs:
                copy.wait_recv()
        own_copies[n].wait()
        for copy in gathers[n][0 if kind == "q" else 1 :]:
            copy.wait_recv()

        def store(there, here, value):
            side.half_s[:, there] = value.astype(bf16)

        product(side, side.other, c0, cw, store)
        cols = pl.ds(c0, cw)
        halves[n] = send(
            side.half_s.at[:, cols], side.half_r.at[:, cols], send_sem.at[n, HALF], recv_sem.at[n, HALF], side.partner
        )

    state_ready = set()

    def adam(n):
        kind, c0, cw = CHUNKS[n]
        side = q if kind == "q" else o
        block = 32 if kind == "q" else 16

        def store(there, here, value):
            side.grad[:, here] = value

        product(side, side.own, c0, cw, store)
        if kind not in state_ready:
            state_ready.add(kind)
            for load in loads[5:8] if kind == "q" else loads[2:5]:
                load.wait()
        halves[n].wait_recv()

        @pl.loop(0, 16)
        def _(b):
            for r in range(0, block, 16):
                rows = pl.ds(pl.multiple_of(b * block + r, 16), 16)
                for c in range(0, cw, min(cw, 512)):
                    cols = pl.ds(c0 + c, min(cw, 512))
                    at = (b // 2, b % 2, pl.ds(r, 16), cols)
                    grad = side.grad[rows, pl.ds(c, min(cw, 512))] + side.half_r[rows, cols].astype(f32)
                    first = first_decay * side.fir[at].astype(f32) + (1.0 - first_decay) * grad
                    second = second_decay * side.sec[at].astype(f32) + (1.0 - second_decay) * grad * grad
                    side.fir[at] = first.astype(bf16)
                    moved = side.off[at] + (first * first_fix) / (jnp.sqrt(second * second_fix) + adam_eps)
                    side.off[at] = moved

        cols = pl.ds(c0, cw)
        cores[n] = send(
            side.off.at[:, 1 - core, :, cols],
            side.core_r.at[:, :, cols],
            send_sem.at[n, CORE],
            recv_sem.at[n, CORE],
            twin,
        )

    def along_z(n):
        kind, c0, cw = CHUNKS[n]
        side = q if kind == "q" else o
        block = 32 if kind == "q" else 16
        cores[n].wait_recv()

        @pl.loop(0, 8)
        def _(b):
            for c in range(0, cw, min(cw, 512)):
                cols = pl.ds(c0 + c, min(cw, 512))
                side.z_s[b % 4, b // 4, :, cols] = (side.off[b, core, :, cols] + side.core_r[b, :, cols]).astype(bf16)

        cols = pl.ds(c0, cw)
        zs[n] = [
            send(
                side.z_s.at[(z + i + 1) % 4, :, :, cols],
                side.z_r.at[i, :, :, cols],
                send_sem.at[n, ZED + i],
                recv_sem.at[n, ZED + i],
                to,
            )
            for i, to in enumerate(zeds)
        ]

    def along_x(n):
        kind, c0, cw = CHUNKS[n]
        side = q if kind == "q" else o
        for copy in zs[n]:
            copy.wait_recv()

        def total(part, cols):
            at = part * 4 + z
            value = side.off[at, core, :, cols] + side.core_r[at, :, cols]
            for i in range(3):
                value = value + side.z_r[i, part, :, cols].astype(f32)
            return value

        for c in range(0, cw, min(cw, 512)):
            cols = pl.ds(c0 + c, min(cw, 512))
            side.x_s[:, cols] = total(1 - xl, cols).astype(bf16)
        cols = pl.ds(c0, cw)
        xs[n] = send(side.x_s.at[:, cols], side.x_r.at[:, cols], send_sem.at[n, XLO], recv_sem.at[n, XLO], near)
        for c in range(0, cw, min(cw, 512)):
            cols = pl.ds(c0 + c, min(cw, 512))
            side.mine[:, cols] = total(xl, cols)

    mom_ready = set()

    def outer(n):
        kind, c0, cw = CHUNKS[n]
        side = q if kind == "q" else o
        if kind not in mom_ready:
            mom_ready.add(kind)
            loads[9 if kind == "q" else 8].wait()
        xs[n].wait_recv()
        for c in range(0, cw, min(cw, 512)):
            cols = pl.ds(c0 + c, min(cw, 512))
            pseudo = (side.mine[:, cols] + side.x_r[:, cols].astype(f32)) / workers
            momentum = outer_mu * side.mom[:, cols] + pseudo
            side.mom[:, cols] = momentum
            side.way[:, cols] = pseudo + outer_mu * momentum

    count = len(CHUNKS)
    gather(0)
    send_q_lhs()
    send_o_lhs()
    for n in range(1, min(AHEAD, count)):
        gather(n)
    for n in range(FORWARD):
        forward(n)
    for step in range(count + max(LATER)):
        if step + AHEAD < count:
            gather(step + AHEAD)
        if step < count:
            partial(step)
        if step + FORWARD < count:
            forward(step + FORWARD)
        for stage, later in zip((adam, along_z, along_x, outer), LATER):
            if 0 <= step - later < count:
                stage(step - later)

    for copy in sent:
        copy.wait_send()


def write_out(*refs):
    sems = refs[12]
    copies = [pltpu.make_async_copy(refs[i], refs[6 + i], sems.at[i]) for i in range(6)]
    for copy in copies:
        copy.start()
    for copy in copies:
        copy.wait()


def per_device(
    tokens_x,
    attn_out,
    query_cot,
    out_cot,
    message_ids,
    q_offset,
    q_first,
    q_second,
    o_offset,
    o_first,
    o_second,
    q_momentum,
    o_momentum,
):
    count = len(CHUNKS)
    any_spec = pl.BlockSpec(memory_space=pl.ANY)

    def side_scratch(rows, cols, chunk):
        block = rows // 16
        return [
            pltpu.VMEM((2, rows, 4 * TOK), bf16),
            pltpu.VMEM((4 * TOK, cols), bf16),
            pltpu.VMEM((rows, cols), bf16),
            pltpu.VMEM((rows, cols), bf16),
            pltpu.VMEM((rows, chunk), f32),
            pltpu.VMEM((8, 2, block, cols), f32),
            pltpu.VMEM((8, 2, block, cols), bf16),
            pltpu.VMEM((8, block, cols), f32),
            pltpu.VMEM((4, 2, block, cols), bf16),
            pltpu.VMEM((3, 2, block, cols), bf16),
            pltpu.VMEM((block, cols), bf16),
            pltpu.VMEM((block, cols), bf16),
            pltpu.VMEM((block, cols), f32),
        ]

    outs = pl.pallas_call(
        kernel,
        out_shape=(
            pltpu.VMEM((8, 2, 32, 2048), bf16),
            pltpu.VMEM((8, 2, 16, 4096), bf16),
            pltpu.VMEM((32, 2048), f32),
            pltpu.VMEM((16, 4096), f32),
            pltpu.VMEM((32, 2048), f32),
            pltpu.VMEM((16, 4096), f32),
        ),
        in_specs=[pl.BlockSpec(memory_space=pltpu.VMEM)] + [any_spec] * 12,
        out_specs=(pl.BlockSpec(memory_space=pltpu.VMEM),) * 6,
        scratch_shapes=[
            pltpu.VMEM((TOK, 4096), bf16),
            pltpu.VMEM((TOK, 2048), bf16),
            pltpu.VMEM((2, 4, 512, TOK), bf16),
            pltpu.VMEM((2, 4, 256, TOK), bf16),
            pltpu.SemaphoreType.DMA((8,)),
            pltpu.SemaphoreType.DMA((8,)),
            pltpu.SemaphoreType.DMA((10,)),
            pltpu.SemaphoreType.DMA((count, N_SEM)),
            pltpu.SemaphoreType.DMA((count, N_SEM)),
            *side_scratch(512, 2048, 512),
            *side_scratch(256, 4096, 1024),
        ],
        compiler_params=pltpu.CompilerParams(
            collective_id=0, has_side_effects=True, vmem_limit_bytes=50 * 2**20
        ),
        cost_estimate=pl.CostEstimate(flops=2**32, bytes_accessed=28 * 2**20, transcendentals=2**22),
        name="diloco",
    )(
        message_ids.reshape(1, TOK),
        tokens_x,
        attn_out,
        query_cot,
        out_cot,
        q_offset.reshape(8, 2, 32, 2048),
        q_first.reshape(8, 2, 32, 2048),
        q_second.reshape(8, 2, 32, 2048),
        o_offset.reshape(8, 2, 16, 4096),
        o_first.reshape(8, 2, 16, 4096),
        o_second.reshape(8, 2, 16, 4096),
        q_momentum,
        o_momentum,
    )
    outs = pl.pallas_call(
        write_out,
        out_shape=tuple(jax.ShapeDtypeStruct(out.shape, out.dtype) for out in outs),
        in_specs=[pl.BlockSpec(memory_space=pltpu.VMEM)] * 6,
        out_specs=(any_spec,) * 6,
        scratch_shapes=[pltpu.SemaphoreType.DMA((6,))],
        compiler_params=pltpu.CompilerParams(vmem_limit_bytes=2**20),
        name="write_out",
    )(*(pltpu.with_memory_space_constraint(out, pltpu.VMEM) for out in outs))
    return (outs[0].reshape(1, 512, 2048), outs[1].reshape(1, 256, 4096), *outs[2:])


def solution(mesh):
    tokens = P(("worker", "fsdp"), None)
    state = P("worker", "fsdp", None)
    share = P(("fsdp", "worker"), None)
    in_specs = (tokens,) * 4 + (P(("worker", "fsdp")),) + (state,) * 6 + (share,) * 2
    out_specs = (state,) * 2 + (share,) * 4
    return jax.shard_map(per_device, mesh=mesh, in_specs=in_specs, out_specs=out_specs, check_vma=False)
```

time: 374 us -> 119 us (0.32)
  waiting for transfers between devices: 235 us -> 0 us
  Pallas kernels: 0 us -> 119 us
  local copies, waits for them, and re-layouts: 47.8 us -> 0 us
  other arithmetic: 34.6 us -> 0 us
  matrix products: 26.4 us -> 0 us
  starting transfers between devices: 14.2 us -> 0 us
  between operations: 14 us -> 0.65 us
    all_gather x2 -> x0, waiting for transfers between devices: 128 us -> none  [the longest x1 87.1 us: per_device(): piece_o = lax.all_gather(o_cot, 'fsdp', axis=0, tiled=True)]
    pallas_call x0 -> x2, Pallas kernels: none -> 119 us  [the longest x1 116 us: per_device(): pl.pallas_call(kernel, out_shape=(pltpu.VMEM((8, 2, 32, 2048), bf16), plt...]
    psum x1 -> x0, waiting for transfers between devices: 107 us -> none  [per_device(): lax.psum(moved_q.astype(jnp.bfloat16), 'worker').astype(jnp.float32)]
    unnamed x41 -> x0, local copies, waits for them, and re-layouts: 45.8 us -> none
    dot_general x16 -> x0, matrix products: 26.4 us -> none  [cross_rows(): lax.dot_general(left, right, (((0,), (0,)), ((), ())), preferred_element_...]
    convert_element_type x3 -> x0, other arithmetic: 16 us -> none  [the longest x1 8.37 us: per_device(): moved_q.astype(jnp.bfloat16)]
    all_to_all x2 -> x0, starting transfers between devices: 14.1 us -> none  [the longest x1 7.48 us: per_device(): lax.all_to_all(tokens_x, 'fsdp', split_axis=1, concat_axis=0, tiled=True)]
    broadcast_in_dim x2 -> x0, other arithmetic: 9.13 us -> none  [the longest x1 4.96 us: per_device(): q_first_new[None]]
  transfers between devices with their start and end apart: 5 -> 0, of which waited for: 3 -> 0; matrix products, arithmetic and copies ran while one was open for 19% -> 0% of each run, Pallas kernels for 0% -> 0%
where the time goes in v1:
time: 119 us
  Pallas kernels  119 us (100%)
    pallas_call x1, Pallas kernels, per_device(): pl.pallas_call(kernel, out_shape=(pltpu.VMEM((8, 2, 32, 2048), bf16), plt...  116 us

profile of v1, /device:TPU:1, one launch (start us, length us, event | category | flops | bytes accessed | tf_op | source)
XLA Modules:
  0.0 119.2 jit_solution(1446699750234492834)
XLA Ops:
  0.6 116.2 %diloco.1 = (bf16[8,2,32,2048]{3,2,1,0:T(8,128)(2,1)S(1)}, bf16[8,2,16,4096]{3,2,1,0:T(8,128)(2,1)S(1)}, f32[32,2048]{1,0:T(8,128)S(1)}, f32[16,4096]{1,0:T(8,12...) custom-call(s32[1,128]{1,0:T(1,128)} %bitcast.15, bf16[128,4096]{1,0:T(8,128)(2,1)} %refs_1_.1, ...), custom_call_target="tpu_custom_call" | custom-call | flops 4294967296 | bytes 29360128 | tf_op jit(solution)/shard_map/diloco/pallas_call | solution.py:395
  116.9 2.4 %write_out.1 = (bf16[8,2,32,2048]{3,2,1,0:T(8,128)(2,1)}, bf16[8,2,16,4096]{3,2,1,0:T(8,128)(2,1)}, f32[32,2048]{1,0:T(8,128)}, f32[16,4096]{1,0:T(8,128)}, f32[32,2048]{1,0:T(8,128)}, /*index=5*/f32[16,4096]{1,0:T(8,128)}) custom-call(bf16[8,2,32,2048]{3,2,1,0:T(8,128)(2,1)S(1)} %get-tuple-element.18.refs_0_, ...), custom_call_target="tpu_custom_call" | custom-call | tf_op jit(solution)/shard_map/write_out/pallas_call | solution.py:440

commit v2 on v1

--- a/solution.py
+++ b/solution.py
@@ -21,13 +21,14 @@
 MESH = pl.DeviceIdType.MESH
 
 CHUNKS = tuple(
-    (kind, number * width, width) for number in range(8) for kind, width in (("q", 256), ("o", 512))
+    (kind, number * width, width, how) for number in range(8) for kind, width, how in (("q", 256, "f"), ("o", 512, "y"))
 )
+CROSS_AHEAD = 12
 AHEAD = 4
 FORWARD = 2
 LATER = (3, 4, 6, 8)
-GATHER, HALF, CORE, ZED, XLO, OWN = 0, 3, 4, 5, 8, 9
-N_SEM = 10
+GATHER, HALF, CORE, ZED, XLO, OWN = 0, 4, 5, 6, 9, 10
+N_SEM = 11
 
 
 class Side:
@@ -100,7 +101,7 @@
             recv_sem.at[number, OWN],
         )
 
-    own_copies = [own_block(q if kind == "q" else o, n, c0, cw) for n, (kind, c0, cw) in enumerate(CHUNKS)]
+    own_copies = [own_block(q if kind == "q" else o, n, c0, cw) for n, (kind, c0, cw, _) in enumerate(CHUNKS)]
     for copy in own_copies:
         copy.start()
     for load in loads[2:]:
@@ -172,37 +173,56 @@
     gathers = {}
     halves, cores, zs, xs = {}, {}, {}, {}
 
-    def gather(n):
-        kind, c0, cw = CHUNKS[n]
+    def gather(n, i):
+        kind, c0, cw, how = CHUNKS[n]
         side = q if kind == "q" else o
         cols = pl.ds(c0, cw)
         src = side.cot_hbm.at[:, cols]
         dst = side.cot.at[pl.ds(pl.multiple_of(side.slot * TOK, TOK), TOK), cols]
-        targets = ring if kind == "q" else (across, beside)
-        gathers[n] = [
-            send(src, dst, send_sem.at[n, GATHER + i], recv_sem.at[n, GATHER + i], to) for i, to in enumerate(targets)
-        ]
+        to = {"d": ring, "f": (ring[0], ring[2])}.get(how, (across, beside))[i]
+        gathers.setdefault(n, []).append(
+            send(src, dst, send_sem.at[n, GATHER + i], recv_sem.at[n, GATHER + i], to)
+        )
+
+    def cross(n):
+        if CHUNKS[n][0] == "o":
+            gather(n, 0)
+
+    def beside_or_ring(n):
+        for i in {"d": (0, 1, 2), "f": (0, 1)}.get(CHUNKS[n][3], (1,)):
+            gather(n, i)
 
     def forward(n):
-        kind, c0, cw = CHUNKS[n]
-        if kind == "q":
+        kind, c0, cw, how = CHUNKS[n]
+        side = q if kind == "q" else o
+        if how == "d":
             return
-        gathers[n][0].wait_recv()
-        slot = (1 - xh) * 2 + y // 2
-        block = o.cot.at[pl.ds(pl.multiple_of(slot * TOK, TOK), TOK), pl.ds(c0, cw)]
-        gathers[n].append(send(block, block, send_sem.at[n, GATHER + 2], recv_sem.at[n, GATHER + 2], beside))
+        if how == "f":
+            passed = [((y + 3) % 4 * TOK, 64, ring[0]), ((y + 1) % 4 * TOK + 64, 64, ring[2])]
+        elif how == "y":
+            passed = [(((1 - xh) * 2 + y // 2) * TOK, TOK, beside)]
+        else:
+            passed = [((xh * 2 + 1 - y // 2) * TOK, TOK, across)]
+        first = 1 if how == "x" else 0
+        for i, (row, rows, to) in enumerate(passed):
+            gathers[n][first + i].wait_recv()
+            block = side.cot.at[pl.ds(pl.multiple_of(row, 64), rows), pl.ds(c0, cw)]
+            at = GATHER + 2 + i
+            gathers[n].append(send(block, block, send_sem.at[n, at], recv_sem.at[n, at], to))
 
     def product(side, which, c0, cw, store):
-        @pl.loop(0, cw // 256)
+        wide = min(cw, 256)
+
+        @pl.loop(0, cw // wide)
         def _(part):
-            there = pl.ds(pl.multiple_of(c0 + part * 256, 256), 256)
-            here = pl.ds(pl.multiple_of(part * 256, 256), 256)
+            there = pl.ds(pl.multiple_of(c0 + part * wide, wide), wide)
+            here = pl.ds(pl.multiple_of(part * wide, wide), wide)
             store(there, here, jnp.dot(side.lhs[which], side.cot[:, there], preferred_element_type=f32))
 
     lhs_ready = set()
 
     def partial(n):
-        kind, c0, cw = CHUNKS[n]
+        kind, c0, cw, how = CHUNKS[n]
         side = q if kind == "q" else o
         if kind not in lhs_ready:
             lhs_ready.add(kind)
@@ -210,7 +230,7 @@
             for copy in q_lhs if kind == "q" else o_lhs:
                 copy.wait_recv()
         own_copies[n].wait()
-        for copy in gathers[n][0 if kind == "q" else 1 :]:
+        for copy in {"d": gathers[n], "f": gathers[n][2:], "y": gathers[n][1:], "x": gathers[n][::2]}[how]:
             copy.wait_recv()
 
         def store(there, here, value):
@@ -225,7 +245,7 @@
     state_ready = set()
 
     def adam(n):
-        kind, c0, cw = CHUNKS[n]
+        kind, c0, cw, how = CHUNKS[n]
         side = q if kind == "q" else o
         block = 32 if kind == "q" else 16
 
@@ -263,7 +283,7 @@
         )
 
     def along_z(n):
-        kind, c0, cw = CHUNKS[n]
+        kind, c0, cw, how = CHUNKS[n]
         side = q if kind == "q" else o
         block = 32 if kind == "q" else 16
         cores[n].wait_recv()
@@ -287,7 +307,7 @@
         ]
 
     def along_x(n):
-        kind, c0, cw = CHUNKS[n]
+        kind, c0, cw, how = CHUNKS[n]
         side = q if kind == "q" else o
         for copy in zs[n]:
             copy.wait_recv()
@@ -311,7 +331,7 @@
     mom_ready = set()
 
     def outer(n):
-        kind, c0, cw = CHUNKS[n]
+        kind, c0, cw, how = CHUNKS[n]
         side = q if kind == "q" else o
         if kind not in mom_ready:
             mom_ready.add(kind)
@@ -325,16 +345,21 @@
             side.way[:, cols] = pseudo + outer_mu * momentum
 
     count = len(CHUNKS)
-    gather(0)
+    cross(0)
+    beside_or_ring(0)
     send_q_lhs()
     send_o_lhs()
-    for n in range(1, min(AHEAD, count)):
-        gather(n)
+    for n in range(1, min(CROSS_AHEAD, count)):
+        cross(n)
+        if n < AHEAD:
+            beside_or_ring(n)
     for n in range(FORWARD):
         forward(n)
     for step in range(count + max(LATER)):
+        if step + CROSS_AHEAD < count:
+            cross(step + CROSS_AHEAD)
         if step + AHEAD < count:
-            gather(step + AHEAD)
+            beside_or_ring(step + AHEAD)
         if step < count:
             partial(step)
         if step + FORWARD < count:

time: 119 us -> 113 us (0.950)
  Pallas kernels: 119 us -> 113 us
    pallas_call x1, Pallas kernels: 116 us -> 110 us  [per_device(): pl.pallas_call(kernel, out_shape=(pltpu.VMEM((8, 2, 32, 2048), bf16), plt...]
where the time goes in v2:
time: 113 us
  Pallas kernels  113 us (100%)
    pallas_call x1, Pallas kernels, per_device(): pl.pallas_call(kernel, out_shape=(pltpu.VMEM((8, 2, 32, 2048), bf16), plt...  110 us
    pallas_call x1, Pallas kernels, per_device(): pl.pallas_call(write_out, out_shape=tuple((jax.ShapeDtypeStruct(out.shape...  2.37 us

profile of v2, /device:TPU:1, one launch (start us, length us, event | category | flops | bytes accessed | tf_op | source)
XLA Modules:
  0.0 113.3 jit_solution(13604298914900363832)
XLA Ops:
  0.6 110.3 %diloco.1 = (bf16[8,2,32,2048]{3,2,1,0:T(8,128)(2,1)S(1)}, bf16[8,2,16,4096]{3,2,1,0:T(8,128)(2,1)S(1)}, f32[32,2048]{1,0:T(8,128)S(1)}, f32[16,4096]{1,0:T(8,12...) custom-call(s32[1,128]{1,0:T(1,128)} %bitcast.15, bf16[128,4096]{1,0:T(8,128)(2,1)} %refs_1_.1, ...), custom_call_target="tpu_custom_call" | custom-call | flops 4294967296 | bytes 29360128 | tf_op jit(solution)/shard_map/diloco/pallas_call | solution.py:420
  110.9 2.4 %write_out.1 = (bf16[8,2,32,2048]{3,2,1,0:T(8,128)(2,1)}, bf16[8,2,16,4096]{3,2,1,0:T(8,128)(2,1)}, f32[32,2048]{1,0:T(8,128)}, f32[16,4096]{1,0:T(8,128)}, f32[32,2048]{1,0:T(8,128)}, /*index=5*/f32[16,4096]{1,0:T(8,128)}) custom-call(bf16[8,2,32,2048]{3,2,1,0:T(8,128)(2,1)S(1)} %get-tuple-element.18.refs_0_, ...), custom_call_target="tpu_custom_call" | custom-call | tf_op jit(solution)/shard_map/write_out/pallas_call | solution.py:465

commit v3 on v2

--- a/solution.py
+++ b/solution.py
@@ -24,7 +24,7 @@
     (kind, number * width, width, how) for number in range(8) for kind, width, how in (("q", 256, "f"), ("o", 512, "y"))
 )
 CROSS_AHEAD = 12
-AHEAD = 4
+AHEAD = 3
 FORWARD = 2
 LATER = (3, 4, 6, 8)
 GATHER, HALF, CORE, ZED, XLO, OWN = 0, 4, 5, 6, 9, 10
@@ -86,8 +86,8 @@
             )
         )
     ]
-    for load in loads[:2]:
-        load.start()
+    loads[1].start()
+    loads[0].start()
 
     barrier = pltpu.get_barrier_semaphore()
     met = (*ring, across, corner, twin, *zeds, near)
@@ -108,19 +108,18 @@
         load.start()
 
     mask = (ids_ref[...] >= CONTROL).astype(f32)
-    loads[0].wait()
-
-    @pl.loop(0, 8)
+
+    def turn(source, target, width, xt, yt):
+        rows = source[:, pl.ds(pl.multiple_of((xt * 4 + yt) * width, width), width)].astype(f32)
+        target[xt, yt] = (rows.T * mask).astype(bf16)
+
+    loads[1].wait()
+
+    @pl.loop(0, 6)
     def _(part):
-        rows = a_in[:, pl.ds(pl.multiple_of(part * 256, 256), 256)].astype(f32)
-        a_t[part // 4, part % 4] = (rows.T * mask).astype(bf16)
-
-    loads[1].wait()
-
-    @pl.loop(0, 8)
-    def _(part):
-        rows = x_in[:, pl.ds(pl.multiple_of(part * 512, 512), 512)].astype(f32)
-        x_t[part // 4, part % 4] = (rows.T * mask).astype(bf16)
+        turn(x_in, x_t, 512, part % 2, (y + 1 + part // 2) % 4)
+
+    pl.semaphore_wait(barrier, len(met))
 
     def lanes(slot):
         return pl.ds(pl.multiple_of(slot * TOK, TOK), TOK)
@@ -129,11 +128,6 @@
         pltpu.make_async_copy(a_t.at[xh, pl.ds(2 * (y // 2), 2)], o.lhs.at[:, :, lanes(o.slot)], lhs_send.at[6]),
         pltpu.make_async_copy(x_t.at[:, y], q.lhs.at[:, :, lanes(q.slot)], lhs_send.at[7]),
     ]
-    for copy in mine:
-        copy.start()
-
-    pl.semaphore_wait(barrier, len(met))
-
     sent = []
 
     def send(src, dst, s, r, to):
@@ -348,6 +342,19 @@
     cross(0)
     beside_or_ring(0)
     send_q_lhs()
+
+    @pl.loop(0, 2)
+    def _(part):
+        turn(x_in, x_t, 512, part, y)
+
+    mine[1].start()
+    loads[0].wait()
+
+    @pl.loop(0, 8)
+    def _(part):
+        turn(a_in, a_t, 256, part // 4, part % 4)
+
+    mine[0].start()
     send_o_lhs()
     for n in range(1, min(CROSS_AHEAD, count)):
         cross(n)

time: 113 us -> 111 us (0.982)
  Pallas kernels: 113 us -> 111 us
    pallas_call x1, Pallas kernels: 110 us -> 108 us  [per_device(): pl.pallas_call(kernel, out_shape=(pltpu.VMEM((8, 2, 32, 2048), bf16), plt...]
where the time goes in v3:
time: 111 us
  Pallas kernels  111 us (100%)
    pallas_call x1, Pallas kernels, per_device(): pl.pallas_call(kernel, out_shape=(pltpu.VMEM((8, 2, 32, 2048), bf16), plt...  108 us
    pallas_call x1, Pallas kernels, per_device(): pl.pallas_call(write_out, out_shape=tuple((jax.ShapeDtypeStruct(out.shape...  2.37 us

profile of v3, /device:TPU:1, one launch (start us, length us, event | category | flops | bytes accessed | tf_op | source)
XLA Modules:
  0.0 111.3 jit_solution(8930516457292846652)
XLA Ops:
  0.6 108.3 %diloco.1 = (bf16[8,2,32,2048]{3,2,1,0:T(8,128)(2,1)S(1)}, bf16[8,2,16,4096]{3,2,1,0:T(8,128)(2,1)S(1)}, f32[32,2048]{1,0:T(8,128)S(1)}, f32[16,4096]{1,0:T(8,12...) custom-call(s32[1,128]{1,0:T(1,128)} %bitcast.15, bf16[128,4096]{1,0:T(8,128)(2,1)} %refs_1_.1, ...), custom_call_target="tpu_custom_call" | custom-call | flops 4294967296 | bytes 29360128 | tf_op jit(solution)/shard_map/diloco/pallas_call | solution.py:427
  108.9 2.4 %write_out.1 = (bf16[8,2,32,2048]{3,2,1,0:T(8,128)(2,1)}, bf16[8,2,16,4096]{3,2,1,0:T(8,128)(2,1)}, f32[32,2048]{1,0:T(8,128)}, f32[16,4096]{1,0:T(8,128)}, f32[32,2048]{1,0:T(8,128)}, /*index=5*/f32[16,4096]{1,0:T(8,128)}) custom-call(bf16[8,2,32,2048]{3,2,1,0:T(8,128)(2,1)S(1)} %get-tuple-element.18.refs_0_, ...), custom_call_target="tpu_custom_call" | custom-call | tf_op jit(solution)/shard_map/write_out/pallas_call | solution.py:472
